TPU v7x, 32 devices: a whole 2x2x4 slice. The times are simulated.
32 devices in a mesh: space: 8 (over y, x, core), wshard: 4 (over z).
Axes of the slice: x: 2, y: 2, z: 4, core: 2. Of those that a mesh axis runs over, the one named last changes fastest.
Arguments:
- features: bfloat16 [32, 64, 4096], P('space'), may hold values from -6 to 6
- weights: bfloat16 [27, 128, 64], P(None, 'wshard'), may hold values from -0.15625 to 0.15625
- gain: float32 [128], P('wshard'), may hold values from 0.1 to 1.9
- cotangent: bfloat16 [32, 128, 4096], P('space', 'wshard'), may hold values from -0.015625 to 0.015625
- counts: int32 [8], P('space'), may hold values from 1 to 4, as said below
- neighbors: int32 [32, 26], P('space'), may hold values from -1 to 31, as said below
Outputs:
- activated: bfloat16 [32, 128, 4096], P('space', 'wshard')
- weight_grad: float32 [27, 128, 64], P(None, 'wshard')
- gain_grad: float32 [128], P('wshard')
Inputs may be any that keep to these rules, and one draw needn't show every extreme that they name: Slots 0 to counts[s] - 1 of index s hold active tiles. Index s and the index half the space axis away form a pair; of each pair one holds at most 2 tiles and the other more than 3. neighbors[t, d] is the global slot (index of space times 4 plus slot) of the active tile at offset d from tile t, or -1 if there is none or t is inactive; the first offset component is the index of space, so a neighbour at dx lies dx indices away.
All inputs are finite; a program needn't handle non-finite values.
Results may differ from a plain program's by a relative error of at most 0.0035.
Values may be sent and summed in bfloat16 or wider, within the bound.
A program may use at most 128 MiB of HBM per device.

v0:
```python
import jax
import jax.numpy as jnp
from jax import lax
from jax.sharding import PartitionSpec as P

TILE = 16


offsets = [
    (along_x, along_y, along_z)
    for along_x in (-1, 0, 1)
    for along_y in (-1, 0, 1)
    for along_z in (-1, 0, 1)
    if (along_x, along_y, along_z) != (0, 0, 0)
]
epsilon = 1e-05


def padded_2(value, sides, width):
    for axis, dim in sides:
        devices, length = (lax.axis_size(axis), value.shape[dim])
        up = [(i, (i + 1) % devices) for i in range(devices - 1)]
        down = [(j, i) for i, j in up]
        last = lax.slice_in_dim(value, length - width, length, axis=dim)
        leading = lax.slice_in_dim(value, 0, width, axis=dim)
        before = lax.ppermute(last, axis, up)
        after = lax.ppermute(leading, axis, down)
        value = jnp.concatenate([before, value, after], axis=dim)
    return value


def source_range(step, size):
    if step < 0:
        return slice(size - 1, size)
    if step > 0:
        return slice(0, 1)
    return slice(0, size)


def target_range(step, size):
    if step < 0:
        return slice(0, 1)
    if step > 0:
        return slice(size + 1, size + 2)
    return slice(1, size + 1)


def conv_cells(block, kernel):
    return lax.conv_general_dilated(
        block,
        kernel,
        (1, 1, 1),
        "VALID",
        dimension_numbers=("NCDHW", "OIDHW", "NCDHW"),
        preferred_element_type=jnp.float32,
    )


def shards(features, weights, gain, cotangent, counts, neighbors):
    slot_count, channels, cell_count = features.shape
    out_local = weights.shape[1]
    edge = TILE
    slot_ids = jnp.arange(slot_count, dtype=jnp.int32)
    active = slot_ids < counts[0]
    tile_cube = jnp.where(active[:, None, None], features, jnp.zeros_like(features)).reshape(
        slot_count, channels, edge, edge, edge
    )
    planes = jnp.stack([tile_cube[:, :, 0], tile_cube[:, :, edge - 1]]).reshape(
        2, slot_count, channels, edge * edge
    )
    beside_all = padded_2(planes, (("space", 0),), 1)
    from_low = beside_all[0].reshape(slot_count, channels, 1, edge, edge)
    from_high = beside_all[3].reshape(slot_count, channels, 1, edge, edge)
    inner_block = jnp.zeros((slot_count, channels, edge, edge + 2, edge + 2), jnp.bfloat16)
    inner_block = inner_block.at[:, :, :, 1:-1, 1:-1].set(tile_cube)
    low_plane = jnp.zeros((slot_count, channels, 1, edge + 2, edge + 2), jnp.bfloat16)
    high_plane = jnp.zeros((slot_count, channels, 1, edge + 2, edge + 2), jnp.bfloat16)
    for number, (along_x, along_y, along_z) in enumerate(offsets):
        if along_x < 0:
            source = from_low
        elif along_x > 0:
            source = from_high
        else:
            source = tile_cube
        piece = source[:, :, :, source_range(along_y, edge), source_range(along_z, edge)]
        column = neighbors[:, number]
        local_slot = jnp.maximum(column, 0) % slot_count
        taken = jnp.take(piece, local_slot, axis=0)
        taken = jnp.where((column >= 0)[:, None, None, None, None], taken, jnp.zeros_like(taken))
        if along_x < 0:
            low_plane = low_plane.at[
                :, :, :, target_range(along_y, edge), target_range(along_z, edge)
            ].set(taken)
        elif along_x > 0:
            high_plane = high_plane.at[
                :, :, :, target_range(along_y, edge), target_range(along_z, edge)
            ].set(taken)
        else:
            inner_block = inner_block.at[
                :, :, :, target_range(along_y, edge), target_range(along_z, edge)
            ].set(taken)
    kernel = weights.reshape(3, 3, 3, out_local, channels).transpose(3, 4, 0, 1, 2)
    padded = jnp.concatenate([low_plane, inner_block, high_plane], axis=2)
    conv_cube = conv_cells(padded, kernel)
    conv_out = conv_cube.reshape(slot_count, out_local, cell_count)
    full_rows = out_local * lax.axis_size("wshard")
    squares = lax.psum(jnp.sum(conv_out * conv_out, axis=1), "wshard")
    inv_rms = lax.rsqrt(squares / full_rows + epsilon)
    scaled = conv_out * inv_rms[:, None, :]
    normed = scaled * gain[None, :, None]
    mask = active.astype(jnp.float32)[:, None, None]
    activated = (jax.nn.silu(normed) * mask).astype(jnp.bfloat16)
    logistic = jax.nn.sigmoid(normed)
    grad_normed = (
        cotangent.astype(jnp.float32) * logistic * (1.0 + normed * (1.0 - logistic)) * mask
    )
    grad_scaled = grad_normed * gain[None, :, None]
    projection = (
        lax.psum(jnp.sum(grad_scaled * scaled, axis=1).astype(jnp.bfloat16), "wshard").astype(
            jnp.float32
        )
        / full_rows
    )
    grad_z = (inv_rms[:, None, :] * (grad_scaled - scaled * projection[:, None, :])).astype(
        jnp.bfloat16
    )
    grad_cube = grad_z.reshape(slot_count, out_local, edge, edge, edge)
    kernel_grad = lax.conv_general_dilated(
        padded,
        grad_cube,
        (1, 1, 1),
        "VALID",
        dimension_numbers=("CNDHW", "IODHW", "NCDHW"),
        preferred_element_type=jnp.float32,
    )
    weight_part = kernel_grad.transpose(2, 3, 4, 1, 0).reshape(27, out_local, channels)
    gain_part = jnp.sum(grad_normed * scaled, axis=(0, 2))
    weight_grad, gain_grad = lax.psum((weight_part, gain_part), "space")
    return (activated, weight_grad, gain_grad)


def solution(mesh):
    placed = (
        P("space", None, None),
        P(None, "wshard", None),
        P("wshard"),
        P("space", "wshard", None),
        P("space"),
        P("space", None),
    )
    return jax.shard_map(
        shards,
        mesh=mesh,
        in_specs=placed,
        out_specs=(P("space", "wshard", None), P(None, "wshard", None), P("wshard")),
        check_vma=False,
    )
```

profile of v0, /device:TPU:0, one launch (start us, length us, event | category | flops | bytes accessed | tf_op | source)
XLA Modules:
  0.0 406.6 jit_solution(10569364923208790066)
XLA Ops:
  8.0 1.8 broadcast_select_fusion.1
  9.8 4.7 %copy.150 = bf16[4,64,4096]{1,0,2:T(4,128)(2,1)} copy(bf16[4,64,4096]{2,1,0:T(8,128)(2,1)S(1)} %broadcast_select_fusion.1) | data formatting | bytes 4194304 | tf_op jit(solution)/shard_map/jit(_where)/select_n | solution.py:65
  17.3 3.0 collective-permute-start
  27.0 4.8 %scatter.105 = bf16[4,64,16,18,18]{1,0,4,3,2:T(4,128)(2,1)} pad(bf16[4,64,16,16,16]{1,0,4,3,2:T(4,128)(2,1)S(1)} %bitcast.252, bf16[]{:T(256)} %constant.889.clone.1), padding=0_0x0_0x0_0x1_1x1_1 | pad | bytes 4751362 | tf_op jit(solution)/shard_map/scatter | solution.py:75
  38.0 2.3 fusion.22
  40.3 3.3 fusion.39
  60.5 2.0 constant_dynamic-update-slice_fusion.5
  64.6 2.0 constant_dynamic-update-slice_fusion.2
  67.3 9.2 %fusion.64 = bf16[64,18,18,4,18]{0,3,4,2,1:T(4,128)(2,1)} fusion(bf16[4,64,1,18,18]{1,0,4,3,2:T(4,128)(2,1)S(1)} %constant_dynamic-update-slice_fusion, bf16[4,64,16,18,18]{1,0,4,3,2:T(4,128)(2,1)} %fusion.34, bf16[4,64,1,18,18]{1,0,4,3,2:T(4,128)(2,1)S(1)} %constant_dynamic-update-slice_fusion.3), kind=kLoop, calls=%fused_computation.319 | loop fusion | flops 2985984 | bytes 5971968 | tf_op jit(solution)/shard_map/concatenate | solution.py:103
  76.6 10.0 %pad.111 = bf16[64,18,18,4,24]{0,3,4,2,1:T(4,128)(2,1)} pad(bf16[64,18,18,4,18]{0,3,4,2,1:T(4,128)(2,1)} %fusion.64, bf16[]{:T(256)} %constant.889.clone.1), padding=0_0x0_0x0_0x0_0x0_6 | pad | bytes 6967298 | tf_op jit(solution)/shard_map/concatenate | solution.py:103
  86.6 4.9 %copy.188 = bf16[64,18,18,4,8,3]{0,4,3,5,2,1:T(8,128)(2,1)S(1)} copy(bf16[64,18,18,4,8,3]{0,3,5,4,2,1:T(4,128)(2,1)} %bitcast.247) | data formatting | bytes 7962624 | tf_op jit(solution)/shard_map/conv_general_dilated | solution.py:49
  93.1 156.9 %multiply_reduce_fusion = (f32[16,16,32,3]{2,3,1,0:T(4,128)}, f32[16,16,32,3,32]{2,4,3,1,0:T(8,128)}) fusion(bf16[3,3,3,32,64]{4,3,2,1,0:T(8,128)(2,1)S(1)} %bitcast.244, bf16[64,18,18,4,7,2]{0,4,3,5,2,1:T(8,128)(2,1)S(1)} %slice.1287, bf16[64,18,18,4,8,3]{0,4,3,5,2,1:T(8,128)(2,1)S(1)} %copy.188, pred[32,3]{0,1:T(4,128)(4,1)S(1)} %copy-done.9), kind=kOutput, calls=%fused_computation.34 | convolution fusion | flops 2740150272 | bytes 9658464 | tf_op jit(solution)/shard_map/conv_general_dilated | solution.py:49
  252.7 13.2 %copy.189 = f32[16,16,32,3,32]{4,1,3,2,0:T(8,128)} copy(f32[16,16,32,3,32]{2,4,3,1,0:T(8,128)} %get-tuple-element.482) | data formatting | bytes 6291456 | tf_op jit(solution)/shard_map/conv_general_dilated | solution.py:49
  265.9 3.9 slice_bitcast_fusion
  269.8 7.1 %copy.190 = f32[4,32,16,16,16]{1,4,3,2,0:T(8,128)} copy(f32[4,32,16,16,16]{1,3,4,0,2:T(8,128)S(1)} %slice_bitcast_fusion) | data formatting | bytes 4194304 | tf_op jit(solution)/shard_map/conv_general_dilated | solution.py:49
  276.9 5.2 %copy.193 = f32[4,32,4096]{2,1,0:T(8,128)S(1)} copy(f32[4,32,4096]{1,2,0:T(8,128)} %bitcast.246) | data formatting | bytes 4194304 | tf_op jit(solution)/shard_map/reshape | solution.py:105
  282.2 7.9 %all-reduce.6.cloned.1.call-done = f32[4,4096]{1,0:T(4,128)} async-done(((f32[4,4096]{1,0:T(4,128)}), f32[4,4096]{1,0:T(4,128)}) %all-reduce.6.cloned.1.call-update) | async-done | bytes 65552 | tf_op jit(solution)/shard_map/psum | solution.py:107
  292.7 18.0 %psum.29 = bf16[4,4096]{1,0:T(4,128)(2,1)S(1)} all-reduce(bf16[4,4096]{1,0:T(4,128)(2,1)S(1)} %get-tuple-element.344), channel_id=1, replica_groups=mesh['space'=8,'wshard'=4] {'wshard'}, use_global_device_ids=true, to_apply=%region_4.12 | all-reduce | flops 16384 | bytes 65536 | tf_op jit(solution)/shard_map/psum | solution.py:119
  310.7 3.7 multiply_convert_fusion
  314.4 3.1 copy.194
  317.5 27.6 %fusion.11 = f32[3,3,3,32,64]{4,3,2,1,0:T(8,128)} fusion(bf16[4,32,16,16,16]{1,4,3,2,0:T(8,128)(2,1)} %bitcast.253, bf16[4,64,1,18,18]{1,0,4,3,2:T(4,128)(2,1)} %copy-done.5, bf16[4,64,16,18,18]{1,0,4,3,2:T(4,128)(2,1)} %fusion.34, bf16[4,64,1,18,18]{1,0,4,3,2:T(4,128)(2,1)} %copy-done.6), kind=kOutput, calls=%fused_computation.39 | convolution fusion | flops 1820897280 | bytes 4255744 | tf_op jit(solution)/shard_map/transpose | solution.py:136
  345.1 12.3 %psum.31 = f32[32]{0:T(128)} all-reduce(f32[32]{0:T(128)S(1)} %get-tuple-element.343), channel_id=1, replica_groups=mesh['space'=8,'wshard'=4] {'space'}, use_global_device_ids=true, to_apply=%region_7.15 | all-reduce | flops 32 | bytes 256 | tf_op jit(solution)/shard_map/psum | solution.py:138
  357.4 40.3 %all-reduce.8.cloned.1.call-done = f32[27,32,64]{2,1,0:T(8,128)} async-done(((f32[27,32,64]{2,1,0:T(8,128)}), f32[27,32,64]{2,1,0:T(8,128)}) %all-reduce.8.cloned.1.call-update) | async-done | bytes 221200 | tf_op jit(solution)/shard_map/psum | solution.py:138
  397.8 1.8 copy.243
  (164 shorter events, 41.5 us)
Async XLA Ops:
  7.2 85.9 %copy-start = (bf16[27,32,64]{2,1,0:T(8,128)(2,1)S(1)}, bf16[27,32,64]{2,1,0:T(8,128)(2,1)}, u32[]{:S(2)}) copy-start(bf16[27,32,64]{2,1,0:T(8,128)(2,1)} %param.75) | copy-start | bytes 331780
  7.2 282.9 %all-reduce.6.cloned.1.call-start = ((), (), s32[]{:S(2)}) async-start(), calls=%async_computation | async-start | bytes 131072 | tf_op jit(solution)/shard_map/psum | solution.py:107
  7.9 12.4 %copy-start.3 = (s32[4,26]{1,0:T(4,128)S(1)}, s32[4,26]{1,0:T(4,128)}, u32[]{:S(2)}) copy-start(s32[4,26]{1,0:T(4,128)} %param.79) | copy-start | bytes 1252
  14.5 12.5 %copy-start.2 = (bf16[4,64,4096]{1,0,2:T(4,128)(2,1)S(1)}, bf16[4,64,4096]{1,0,2:T(4,128)(2,1)}, u32[]{:S(2)}) copy-start(bf16[4,64,4096]{1,0,2:T(4,128)(2,1)} %copy.150) | copy-start | bytes 6291460
  15.9 32.4 %collective-permute-start.1 = (bf16[1,4,64,256]{2,1,3,0:T(4,128)(2,1)S(1)}, bf16[1,4,64,256]{2,1,3,0:T(4,128)(2,1)S(1)}, u32[]{:S(2)}, u32[]{:S(2)}) collective-permute-start(bf16[1,4,64,256]{2,1,3,0:T(4,128)(2,1)S(1)} %bitcast.265), channel_id=1, source_target_pairs={{4,0},{8,4},{12,8},{16,12},{20,16},{24,20},{28,24},{5,1},{9,5},{13... | collective-permute-start | bytes 393224 | tf_op jit(solution)/shard_map/ppermute | solution.py:27
  17.3 31.0 %collective-permute-start = (bf16[1,4,64,256]{2,1,3,0:T(4,128)(2,1)S(1)}, bf16[1,4,64,256]{2,1,3,0:T(4,128)(2,1)S(1)}, u32[]{:S(2)}, u32[]{:S(2)}) collective-permute-start(bf16[1,4,64,256]{2,1,3,0:T(4,128)(2,1)S(1)} %bitcast.264), channel_id=1, source_target_pairs={{0,4},{4,8},{8,12},{12,16},{16,20},{20,24},{24,28},{1,5},{5,9},{9,... | collective-permute-start | bytes 393224 | tf_op jit(solution)/shard_map/ppermute | solution.py:26
  26.9 5.0 %copy-start.8 = (s32[5]{0:T(128)S(1)}, s32[5]{0:T(128)}, u32[]{:S(2)}) copy-start(s32[5]{0:T(128)} %constant.894.clone.1) | copy-start | bytes 64
  63.3 13.3 %copy-start.6 = (bf16[4,64,1,18,18]{1,0,4,3,2:T(4,128)(2,1)}, bf16[4,64,1,18,18]{1,0,4,3,2:T(4,128)(2,1)S(1)}, u32[]{:S(2)}) copy-start(bf16[4,64,1,18,18]{1,0,4,3,2:T(4,128)(2,1)S(1)} %constant_dynamic-update-slice_fusion.3) | copy-start | bytes 497668
  67.3 9.2 %copy-start.5 = (bf16[4,64,1,18,18]{1,0,4,3,2:T(4,128)(2,1)}, bf16[4,64,1,18,18]{1,0,4,3,2:T(4,128)(2,1)S(1)}, u32[]{:S(2)}) copy-start(bf16[4,64,1,18,18]{1,0,4,3,2:T(4,128)(2,1)S(1)} %constant_dynamic-update-slice_fusion) | copy-start | bytes 497668
  91.5 1.5 copy-start.9
  252.6 145.1 %all-reduce.8.cloned.1.call-start = ((), (), s32[]{:S(2)}) async-start(), calls=%async_computation.1 | async-start | bytes 884736 | tf_op jit(solution)/shard_map/psum | solution.py:138
  276.9 14.1 %copy-start.4 = (bf16[4,32,4096]{2,1,0:T(8,128)(2,1)S(1)}, bf16[4,32,4096]{2,1,0:T(8,128)(2,1)}, u32[]{:S(2)}) copy-start(bf16[4,32,4096]{2,1,0:T(8,128)(2,1)} %param.77) | copy-start | bytes 3145732
  276.9 14.1 %copy-start.7 = (f32[32]{0:T(128)S(1)}, f32[32]{0:T(128)}, u32[]{:S(2)}) copy-start(f32[32]{0:T(128)} %param.76) | copy-start | bytes 388
  317.5 82.1 %copy-start.1 = (bf16[27,32,64]{2,1,0:T(8,128)(2,1)S(1)}, bf16[27,32,64]{2,1,0:T(8,128)(2,1)}, u32[]{:S(2)}) copy-start(bf16[27,32,64]{2,1,0:T(8,128)(2,1)} %param.75) | copy-start | bytes 331780
Sparse Core Ops, SparseCore 0:
  252.8 37.3 all-reduce.5
  345.2 52.4 all-reduce.7
where the time goes:
time: 414 us; the launch traced here: 407 us
  matrix products  184 us (44%)
  local copies, waits for them, and re-layouts  84.3 us (20%)
  waiting for transfers between devices  48.3 us (12%)
  other arithmetic  38.8 us (9%)
  blocking collectives  30.3 us (7%)
  between operations  15.8 us (4%)
  starting transfers between devices  4.55 us (1%)
    conv_general_dilated x1, matrix products, conv_cells(): lax.conv_general_dilated(block, kernel, (1, 1, 1), 'VALID', dimension_num...  157 us
    psum x1, waiting for transfers between devices, shards(): weight_grad, gain_grad = lax.psum((weight_part, gain_part), 'space')  40.3 us
    conv_general_dilated x5, local copies, waits for them, and re-layouts, conv_cells(): lax.conv_general_dilated(block, kernel, (1, 1, 1), 'VALID', dimension_num...  30.6 us
    transpose x1, matrix products, shards(): kernel_grad.transpose(2, 3, 4, 1, 0).reshape(27, out_local, channels)  27.6 us
    psum x1, blocking collectives, shards(): lax.psum(jnp.sum(grad_scaled * scaled, axis=1).astype(jnp.bfloat16), 'wsh...  18 us
    gather x26, local copies, waits for them, and re-layouts, shards(): taken = jnp.take(piece, local_slot, axis=0)  14.8 us
    psum x1, blocking collectives, shards(): weight_grad, gain_grad = lax.psum((weight_part, gain_part), 'space')  12.3 us
    scatter x8, other arithmetic, shards(): inner_block = inner_block.at[:, :, :, target_range(along_y, edge), target...  10.6 us
  transfers between devices with their start and end apart: 4, of which 2 were waited for; matrix products, arithmetic and copies ran while one was open for 14% of the time, Pallas kernels for 0%

commit v1 on v0

v1 whole, which is shorter than its diff:
```python
import functools

import jax
import jax.numpy as jnp
import numpy as np
from jax import lax
from jax.experimental import pallas as pl
from jax.experimental.pallas import tpu as pltpu
from jax.sharding import PartitionSpec as P

TILE = 16
PLANE = TILE * TILE
epsilon = 1e-05
MESH = pl.DeviceIdType.MESH
LANES = 128
BF = jnp.bfloat16
F32 = jnp.float32


def shift_tables():
    perms = np.zeros((9, PLANE, PLANE), np.float32)
    for j in range(9):
        dy, dz = j // 3 - 1, j % 3 - 1
        for y in range(TILE):
            for z in range(TILE):
                source = ((y + dy) % TILE) * TILE + (z + dz) % TILE
                perms[j, source, y * TILE + z] = 1.0
    masks = np.zeros((4, TILE, PLANE), np.float32)
    lane = np.arange(PLANE)
    masks[0] = lane // TILE == 0
    masks[1] = lane // TILE == TILE - 1
    masks[2] = lane % TILE == 0
    masks[3] = lane % TILE == TILE - 1
    return perms, masks


def picked(load, j, masks):
    dy, dz = j // 3 - 1, j % 3 - 1
    value = load(4)
    wide = value.shape
    mask_y = jnp.broadcast_to(masks[0 if dy > 0 else 1][None, :1], wide) > 0
    mask_z = jnp.broadcast_to(masks[2 if dz > 0 else 3][None, :1], wide) > 0
    if dz:
        value = jnp.where(mask_z, load(3 + dz + 1), value)
    if dy:
        beside = load((dy + 1) * 3 + 1)
        if dz:
            beside = jnp.where(mask_z, load(j), beside)
        value = jnp.where(mask_y, beside, value)
    return value


def kernel(
    n_space, n_w, idx, act, feat, w96, gain, cot, perms, masks,
    out, red_out,
    src, edge, sendp, x9, part, conv, sq, inv, pf, pb, ptot, gz, acc, gacc, red, rbuf, full,
    halo_send, halo_recv, sq_send, sq_recv, pb_send, pb_recv, rs_send, rs_recv, ag_send, ag_recv,
):
    slots, channels, _ = feat.shape
    rows_out = cot.shape[1]
    me_s = lax.axis_index("space")
    me_w = lax.axis_index("wshard")
    taps = 9 * channels
    chunk = red.shape[0] // n_space

    barrier = pltpu.get_barrier_semaphore()

    def greet_space(d, c):
        pl.semaphore_signal(
            barrier, inc=1, device_id=(lax.rem(me_s + d, n_space), me_w), device_id_type=MESH
        )
        return c

    def greet_w(d, c):
        pl.semaphore_signal(
            barrier, inc=1, device_id=(me_s, lax.rem(me_w + d, n_w)), device_id_type=MESH
        )
        return c

    lax.fori_loop(1, n_space, greet_space, 0)
    lax.fori_loop(1, n_w, greet_w, 0)

    for s in range(slots):
        sendp[0, s] = feat[s, :, (TILE - 1) * PLANE :]
        sendp[1, s] = feat[s, :, :PLANE]
    pl.semaphore_wait(barrier, n_space - 1 + n_w - 1)

    def halo(side):
        step = 1 if side == 0 else n_space - 1
        return pltpu.make_async_remote_copy(
            src_ref=sendp.at[side],
            dst_ref=edge.at[side, pl.ds(0, slots)],
            send_sem=halo_send.at[side],
            recv_sem=halo_recv.at[side],
            device_id=(lax.rem(me_s + step, n_space), me_w),
            device_id_type=MESH,
        )

    for side in range(2):
        halo(side).start()

    for side in range(2):
        edge[side, slots] = jnp.zeros((channels, PLANE), BF)

    def fill(x, c):
        lanes = pl.ds(pl.multiple_of(x * PLANE, PLANE), PLANE)
        for s in range(slots):
            src[s, x] = feat[s, :, lanes]
        src[slots, x] = jnp.zeros((channels, PLANE), BF)
        return c

    lax.fori_loop(0, TILE, fill, 0)
    acc[...] = jnp.zeros_like(acc)
    gacc[...] = jnp.zeros_like(gacc)

    GROUP = 4

    def inner_cells(t, c):
        for j in range(9):
            def some(g, c, j=j):
                def load(k):
                    return src[idx[t, 9 + k], pl.ds(g * GROUP, GROUP)]

                value = picked(load, j, masks)
                if j != 4:
                    value = jnp.dot(
                        value.reshape(GROUP * channels, PLANE), perms[j], preferred_element_type=F32
                    ).astype(BF).reshape(GROUP, channels, PLANE)
                x9[t, pl.ds(1 + g * GROUP, GROUP), j * channels : (j + 1) * channels] = value
                return c

            lax.fori_loop(0, TILE // GROUP, some, 0)
        return c

    lax.fori_loop(0, slots, inner_cells, 0)

    for side in range(2):
        halo(side).wait()

    def squares(t, d):
        return pltpu.make_async_remote_copy(
            src_ref=sq.at[0, t],
            dst_ref=sq.at[d, t],
            send_sem=sq_send.at[t, d],
            recv_sem=sq_recv.at[t, d],
            device_id=(me_s, lax.rem(me_w + d, n_w)),
            device_id_type=MESH,
        )

    def sums(t, d):
        return pltpu.make_async_remote_copy(
            src_ref=pb.at[0, t],
            dst_ref=pb.at[d, t],
            send_sem=pb_send.at[t, d],
            recv_sem=pb_recv.at[t, d],
            device_id=(me_s, lax.rem(me_w + d, n_w)),
            device_id_type=MESH,
        )

    def forward(t, c):
        for j in range(9):
            values = []
            for side in range(2):
                def load(k, side=side):
                    return edge[side, idx[t, 18 * side + k]][None]

                values.append(picked(load, j, masks))
            value = jnp.concatenate(values, axis=0).reshape(2 * channels, PLANE)
            if j != 4:
                value = jnp.dot(value, perms[j], preferred_element_type=F32).astype(BF)
            x9[t, 0, j * channels : (j + 1) * channels] = value[:channels]
            x9[t, TILE + 1, j * channels : (j + 1) * channels] = value[channels:]

        def layer(x, c):
            part[x] = jnp.dot(w96[...], x9[t, x], preferred_element_type=F32)
            return c

        lax.fori_loop(0, TILE + 2, layer, 0, unroll=2)

        def combine(x, c):
            value = (
                part[x, :rows_out]
                + part[x + 1, rows_out : 2 * rows_out]
                + part[x + 2, 2 * rows_out :]
            )
            conv[t, x] = value
            sq[0, t, pl.ds(x, 1)] = jnp.sum(value * value, axis=0, keepdims=True)
            return c

        lax.fori_loop(0, TILE, combine, 0, unroll=2)
        for d in range(1, n_w):
            squares(t, d).start()
        return c

    lax.fori_loop(0, slots, forward, 0)

    full_rows = rows_out * n_w
    gain_wide = jnp.broadcast_to(gain[...], (rows_out, PLANE))

    def cell_terms(t, x):
        lanes = pl.ds(pl.multiple_of(x * PLANE, PLANE), PLANE)
        row = inv[t, pl.ds(x, 1)]
        scaled = conv[t, x] * row
        normed = scaled * gain_wide
        s = jax.nn.sigmoid(normed)
        grad = cot[t, :, lanes].astype(F32) * s * (1.0 + normed * (1.0 - s)) * act[t]
        return lanes, row, scaled, normed, s, grad

    def middle(t, c):
        for d in range(1, n_w):
            squares(t, d).wait()
        total = sq[0, t]
        for d in range(1, n_w):
            total = total + sq[d, t]
        inv[t] = lax.rsqrt(total / full_rows + epsilon)

        def cells(x, c):
            lanes, row, scaled, normed, s, grad = cell_terms(t, x)
            out[t, :, lanes] = (normed * s * act[t]).astype(BF)
            gacc[...] += grad * scaled
            grad_scaled = grad * gain_wide
            pf[pl.ds(x, 1)] = jnp.sum(grad_scaled * scaled, axis=0, keepdims=True)
            return c

        lax.fori_loop(0, TILE, cells, 0, unroll=2)
        pb[0, t] = pf[...].astype(BF)
        for d in range(1, n_w):
            sums(t, d).start()
        return c

    lax.fori_loop(0, slots, middle, 0)

    for m in (0, 1, TILE + 2, TILE + 3):
        gz[m] = jnp.zeros((rows_out, PLANE), BF)

    def backward(t, c):
        for d in range(1, n_w):
            sums(t, d).wait()
        total = pb[0, t].astype(F32)
        for d in range(1, n_w):
            total = total + pb[d, t].astype(F32)
        ptot[...] = total / full_rows

        def cells(x, c):
            lanes, row, scaled, normed, s, grad = cell_terms(t, x)
            value = row * (grad * gain_wide - scaled * ptot[pl.ds(x, 1)])
            gz[x + 2] = value.astype(BF)
            return c

        lax.fori_loop(0, TILE, cells, 0, unroll=2)

        def layer(x, c):
            left = gz[pl.ds(x, 3)].reshape(3 * rows_out, PLANE)
            acc[...] += lax.dot_general(
                left, x9[t, x], (((1,), (1,)), ((), ())), preferred_element_type=F32
            )
            return c

        lax.fori_loop(0, TILE + 2, layer, 0, unroll=2)
        return c

    lax.fori_loop(0, slots, backward, 0)

    rows = 3 * rows_out
    blocks = (taps + LANES - 1) // LANES
    for b in range(blocks):
        width = min(LANES, taps - b * LANES)
        value = acc[:, b * LANES : b * LANES + width]
        if width < LANES:
            red[b * rows : (b + 1) * rows] = jnp.zeros((rows, LANES), F32)
            red[b * rows : (b + 1) * rows, :width] = value
        else:
            red[b * rows : (b + 1) * rows] = value
    at = blocks * rows
    red[at : at + rows_out] = jnp.broadcast_to(
        jnp.sum(gacc[...], axis=1, keepdims=True), (rows_out, LANES)
    )
    if red.shape[0] > at + rows_out:
        red[at + rows_out :] = jnp.zeros((red.shape[0] - at - rows_out, LANES), F32)

    def piece(ref, index):
        return ref.at[pl.ds(pl.multiple_of(index * chunk, 8), chunk)]

    def scatter(d):
        peer = lax.rem(me_s + d, n_space)
        return pltpu.make_async_remote_copy(
            src_ref=piece(red, peer),
            dst_ref=rbuf.at[d],
            send_sem=rs_send.at[d],
            recv_sem=rs_recv.at[d],
            device_id=(peer, me_w),
            device_id_type=MESH,
        )

    def gather(d, index):
        return pltpu.make_async_remote_copy(
            src_ref=piece(full, index),
            dst_ref=piece(full, index),
            send_sem=ag_send.at[d],
            recv_sem=ag_recv.at[d],
            device_id=(lax.rem(me_s + d, n_space), me_w),
            device_id_type=MESH,
        )

    def each(first):
        def body(d, c):
            first(d)
            return c

        lax.fori_loop(1, n_space, body, 0)

    each(lambda d: scatter(d).start())
    mine = pl.ds(pl.multiple_of(me_s * chunk, 8), chunk)
    rbuf[0] = red[mine]

    def arrived(d):
        scatter(d).wait_recv()
        rbuf[0] += rbuf[d]

    each(arrived)
    full[mine] = rbuf[0]
    each(lambda d: gather(d, me_s).start())
    each(lambda d: gather(d, lax.rem(me_s + n_space - d, n_space)).wait_recv())
    each(lambda d: scatter(d).wait_send())
    each(lambda d: gather(d, me_s).wait_send())
    red_out[...] = full[...]


def shards(features, weights, gain, cotangent, counts, neighbors):
    slots, channels, cells = features.shape
    rows_out = weights.shape[1]
    n_space, n_w = lax.axis_size("space"), lax.axis_size("wshard")
    slot_ids = jnp.arange(slots, dtype=jnp.int32)
    active = slot_ids < counts[0]
    local = jnp.where(neighbors >= 0, neighbors % slots, slots)
    own = jnp.where(active, slot_ids, slots)[:, None]
    idx = jnp.concatenate([local[:, :13], own, local[:, 13:]], axis=1).astype(jnp.int32)
    w96 = weights.reshape(3, 9, rows_out, channels).transpose(0, 2, 1, 3).reshape(
        3 * rows_out, 9 * channels
    )
    perms, masks = shift_tables()
    rows = 3 * rows_out
    blocks = (9 * channels + LANES - 1) // LANES
    used = blocks * rows + rows_out
    red_rows = -(-used // (8 * n_space)) * 8 * n_space
    vmem = pl.BlockSpec(memory_space=pltpu.VMEM)
    smem = pl.BlockSpec(memory_space=pltpu.SMEM)
    dma = pltpu.SemaphoreType.DMA
    out, red = pl.pallas_call(
        functools.partial(kernel, n_space, n_w),
        out_shape=(
            jax.ShapeDtypeStruct((slots, rows_out, cells), BF),
            jax.ShapeDtypeStruct((red_rows, LANES), F32),
        ),
        in_specs=[smem, smem, vmem, vmem, vmem, vmem, vmem, vmem],
        out_specs=(vmem, vmem),
        scratch_shapes=[
            pltpu.VMEM((slots + 1, TILE, channels, PLANE), BF),
            pltpu.VMEM((2, slots + 1, channels, PLANE), BF),
            pltpu.VMEM((2, slots, channels, PLANE), BF),
            pltpu.VMEM((slots, TILE + 2, 9 * channels, PLANE), BF),
            pltpu.VMEM((TILE + 2, rows, PLANE), F32),
            pltpu.VMEM((slots, TILE, rows_out, PLANE), F32),
            pltpu.VMEM((n_w, slots, TILE, PLANE), F32),
            pltpu.VMEM((slots, TILE, PLANE), F32),
            pltpu.VMEM((TILE, PLANE), F32),
            pltpu.VMEM((n_w, slots, TILE, PLANE), BF),
            pltpu.VMEM((TILE, PLANE), F32),
            pltpu.VMEM((TILE + 4, rows_out, PLANE), BF),
            pltpu.VMEM((rows, 9 * channels), F32),
            pltpu.VMEM((rows_out, PLANE), F32),
            pltpu.VMEM((red_rows, LANES), F32),
            pltpu.VMEM((n_space, red_rows // n_space, LANES), F32),
            pltpu.VMEM((red_rows, LANES), F32),
            dma((2,)), dma((2,)),
            dma((slots, n_w)), dma((slots, n_w)),
            dma((slots, n_w)), dma((slots, n_w)),
            dma((n_space,)), dma((n_space,)),
            dma((n_space,)), dma((n_space,)),
        ],
        compiler_params=pltpu.CompilerParams(
            collective_id=0, has_side_effects=True, vmem_limit_bytes=56 * 1024 * 1024
        ),
    )(
        idx, active.astype(F32), features, w96, gain.reshape(rows_out, 1), cotangent,
        jnp.asarray(perms, BF), jnp.asarray(masks, BF),
    )
    taken = red[: blocks * rows].reshape(blocks, 3, rows_out, LANES)[:, ::-1]
    taken = taken.transpose(1, 2, 0, 3).reshape(3, rows_out, blocks * LANES)[:, :, : 9 * channels]
    weight_grad = taken.reshape(3, rows_out, 9, channels).transpose(0, 2, 1, 3).reshape(
        27, rows_out, channels
    )
    gain_grad = red[blocks * rows : blocks * rows + rows_out, 0]
    return (out, weight_grad, gain_grad)


def solution(mesh):
    placed = (
        P("space", None, None),
        P(None, "wshard", None),
        P("wshard"),
        P("space", "wshard", None),
        P("space"),
        P("space", None),
    )
    return jax.shard_map(
        shards,
        mesh=mesh,
        in_specs=placed,
        out_specs=(P("space", "wshard", None), P(None, "wshard", None), P("wshard")),
        check_vma=False,
    )
```

time: 414 us -> 83.7 us (0.20); the launches traced: 407 us -> 83.5 us
  matrix products: 184 us -> 0 us
  local copies, waits for them, and re-layouts: 84.3 us -> 7.9 us
  Pallas kernels: 0 us -> 72.3 us
  waiting for transfers between devices: 48.3 us -> 0 us
  other arithmetic: 38.8 us -> 1.93 us
  blocking collectives: 30.3 us -> 0 us
  between operations: 15.8 us -> 1.33 us
  starting transfers between devices: 4.55 us -> 0 us
    conv_general_dilated x1 -> x0, matrix products: 157 us -> none  [conv_cells(): lax.conv_general_dilated(block, kernel, (1, 1, 1), 'VALID', dimension_num...]
    pallas_call x0 -> x1, Pallas kernels: none -> 72.3 us  [shards(): pl.pallas_call(functools.partial(kernel, n_space, n_w), out_shape=(jax.Sh...]
    psum x2 -> x0, waiting for transfers between devices: 48.3 us -> none  [the longest x1 40.3 us: shards(): weight_grad, gain_grad = lax.psum((weight_part, gain_part), 'space')]
    conv_general_dilated x5 -> x0, local copies, waits for them, and re-layouts: 30.6 us -> none  [conv_cells(): lax.conv_general_dilated(block, kernel, (1, 1, 1), 'VALID', dimension_num...]
    psum x2 -> x0, blocking collectives: 30.3 us -> none  [the longest x1 18 us: shards(): lax.psum(jnp.sum(grad_scaled * scaled, axis=1).astype(jnp.bfloat16), 'wsh...]
    transpose x1 -> x0, matrix products: 27.6 us -> none  [shards(): kernel_grad.transpose(2, 3, 4, 1, 0).reshape(27, out_local, channels)]
    scatter x24 -> x0, other arithmetic: 18.8 us -> none  [the longest x8 10.6 us: shards(): inner_block = inner_block.at[:, :, :, target_range(along_y, edge), target...]
    gather x26 -> x0, local copies, waits for them, and re-layouts: 14.8 us -> none  [shards(): taken = jnp.take(piece, local_slot, axis=0)]
  transfers between devices with their start and end apart: 4 -> 0, of which waited for: 2 -> 0; matrix products, arithmetic and copies ran while one was open for 14% -> 0% of each run, Pallas kernels for 0% -> 0%
where the time goes in v1:
time: 83.7 us; the launch traced here: 83.5 us
  Pallas kernels  72.3 us (86%)
  local copies, waits for them, and re-layouts  7.9 us (9%)
  other arithmetic  1.93 us (2%)
  between operations  1.33 us (2%)
    pallas_call x1, Pallas kernels, shards(): pl.pallas_call(functools.partial(kernel, n_space, n_w), out_shape=(jax.Sh...  72.3 us
    reshape x2, local copies, waits for them, and re-layouts, shards(): weights.reshape(3, 9, rows_out, channels).transpose(0, 2, 1, 3)  1.94 us

profile of v1, /device:TPU:0, one launch (start us, length us, event | category | flops | bytes accessed | tf_op | source)
XLA Modules:
  0.0 83.5 jit_solution(12127628228070112906)
XLA Ops:
  1.3 0.6 compare_convert_fusion.act
  1.9 0.7 fusion.1
  2.6 0.1 fusion.2
  2.6 0.7 pad_add_fusion.idx
  3.3 1.3 %copy.17.gain = f32[32,1]{1,0:T(8,128)} copy(f32[32,1]{0,1:T(1,128)} %bitcast.20) | data formatting | bytes 256 | tf_op jit(solution)/shard_map/reshape | solution.py:385
  4.6 1.0 %copy.21 = bf16[3,9,32,64]{3,1,2,0:T(8,128)(2,1)S(1)} copy(bf16[3,9,32,64]{3,2,1,0:T(8,128)(2,1)} %bitcast.19) | data formatting | bytes 221184 | tf_op jit(solution)/shard_map/reshape | solution.py:338
  5.7 0.9 %reshape.41.w96 = bf16[96,576]{1,0:T(8,128)(2,1)} reshape(bf16[3,32,9,64]{3,2,1,0:T(8,128)(2,1)S(1)} %bitcast.15) | data formatting | bytes 221184 | tf_op jit(solution)/shard_map/reshape | solution.py:338
  6.6 72.3 %shard_map.103 = (bf16[4,32,4096]{2,1,0:T(8,128)(2,1)}, f32[512,128]{1,0:T(8,128)}) custom-call(s32[4,27]{1,0:T(4,128)} %pad_add_fusion.idx, f32[4]{0:T(128)} %compare_convert_fusion.act, bf16[4,64,4096]{2,1,0:T(8,128)(2,1)} %feat.1, bf16[96,576]{1,0:T(8,128)(2,1)} %reshape.41.w96, f32[32,1]{1,0:T(8,128)} %copy.17.gain, bf16[4,32,4096]{2,1,0:T(8,128)(2,1)} %cot.1, ...), custom_call_target="tpu_custom_call" | custom-call | tf_op jit(solution)/shard_map/pallas_call | solution.py:349
  78.9 1.3 %slice_reduce_fusion = f32[32]{0:T(128)} fusion(f32[512,128]{1,0:T(8,128)} %get-tuple-element.6), kind=kLoop, calls=%fused_computation.2 | loop fusion | bytes 256 | tf_op jit(solution)/shard_map/slice | solution.py:393
  80.2 1.0 %slice.17 = f32[480,128]{1,0:T(8,128)S(1)} slice(f32[512,128]{1,0:T(8,128)} %get-tuple-element.6), slice={[0:480], [0:128]} | slice | bytes 491520 | tf_op jit(solution)/shard_map/slice | solution.py:388
  81.2 0.0 copy-start
  81.2 0.1 copy.18
  81.4 0.1 reshape.44
  81.4 0.1 reshape.45
  81.6 0.9 %copy.19 = f32[3,9,32,64]{3,2,1,0:T(8,128)} copy(f32[3,9,32,64]{3,1,2,0:T(8,128)S(1)} %bitcast.14) | data formatting | bytes 442368 | tf_op jit(solution)/shard_map/transpose | solution.py:390
  82.5 0.0 copy-done
  82.5 1.0 %copy.24 = bf16[4,32,4096]{2,1,0:T(8,128)(2,1)} copy(bf16[4,32,4096]{2,1,0:T(8,128)(2,1)S(1)} %copy-done) | data formatting | bytes 2097152
  (2 shorter events, 0.0 us)
Async XLA Ops:
  81.2 1.3 %copy-start = (bf16[4,32,4096]{2,1,0:T(8,128)(2,1)S(1)}, bf16[4,32,4096]{2,1,0:T(8,128)(2,1)}, u32[]{:S(2)}) copy-start(bf16[4,32,4096]{2,1,0:T(8,128)(2,1)} %get-tuple-element.12) | copy-start | bytes 3145732

commit v2 on v1

--- a/solution.py
+++ b/solution.py
@@ -51,9 +51,9 @@
 
 
 def kernel(
-    n_space, n_w, idx, act, feat, w96, gain, cot, perms, masks,
-    out, red_out,
-    src, edge, sendp, x9, part, conv, sq, inv, pf, pb, ptot, gz, acc, gacc, red, rbuf, full,
+    n_space, n_w, neighbors, counts, feat, weights, gain, cot, perms, masks,
+    out, weight_out, gain_out,
+    w96, src, edge, sendp, x9, part, conv, sq, inv, pf, pb, ptot, gz, acc, gacc, red, rbuf, full,
     halo_send, halo_recv, sq_send, sq_recv, pb_send, pb_recv, rs_send, rs_recv, ag_send, ag_recv,
 ):
     slots, channels, _ = feat.shape
@@ -61,6 +61,16 @@
     me_s = lax.axis_index("space")
     me_w = lax.axis_index("wshard")
     taps = 9 * channels
+
+    def slot(t, k):
+        if k == 13:
+            return jnp.where(t < counts[0], t, slots)
+        found = neighbors[t, k - (k > 13)]
+        return jnp.where(found >= 0, lax.rem(found, slots), slots)
+
+    def live(t):
+        return jnp.where(t < counts[0], 1.0, 0.0).astype(F32)
+
     chunk = red.shape[0] // n_space
 
     barrier = pltpu.get_barrier_semaphore()
@@ -110,16 +120,19 @@
         return c
 
     lax.fori_loop(0, TILE, fill, 0)
+    for k in range(27):
+        dx, j = k // 9, k % 9
+        w96[dx * rows_out : (dx + 1) * rows_out, j * channels : (j + 1) * channels] = weights[k]
     acc[...] = jnp.zeros_like(acc)
     gacc[...] = jnp.zeros_like(gacc)
 
-    GROUP = 4
+    GROUP = 16
 
     def inner_cells(t, c):
         for j in range(9):
             def some(g, c, j=j):
                 def load(k):
-                    return src[idx[t, 9 + k], pl.ds(g * GROUP, GROUP)]
+                    return src[slot(t, 9 + k), pl.ds(g * GROUP, GROUP)]
 
                 value = picked(load, j, masks)
                 if j != 4:
@@ -136,6 +149,24 @@
 
     for side in range(2):
         halo(side).wait()
+
+    for j in range(9):
+        values = []
+        for t in range(slots):
+            for side in range(2):
+                def load(k, t=t, side=side):
+                    return edge[side, slot(t, 18 * side + k)][None]
+
+                values.append(picked(load, j, masks))
+        value = jnp.concatenate(values, axis=0).reshape(2 * slots * channels, PLANE)
+        if j != 4:
+            value = jnp.dot(value, perms[j], preferred_element_type=F32).astype(BF)
+        for t in range(slots):
+            for side in range(2):
+                start = (2 * t + side) * channels
+                x9[t, side * (TILE + 1), j * channels : (j + 1) * channels] = value[
+                    start : start + channels
+                ]
 
     def squares(t, d):
         return pltpu.make_async_remote_copy(
@@ -158,19 +189,6 @@
         )
 
     def forward(t, c):
-        for j in range(9):
-            values = []
-            for side in range(2):
-                def load(k, side=side):
-                    return edge[side, idx[t, 18 * side + k]][None]
-
-                values.append(picked(load, j, masks))
-            value = jnp.concatenate(values, axis=0).reshape(2 * channels, PLANE)
-            if j != 4:
-                value = jnp.dot(value, perms[j], preferred_element_type=F32).astype(BF)
-            x9[t, 0, j * channels : (j + 1) * channels] = value[:channels]
-            x9[t, TILE + 1, j * channels : (j + 1) * channels] = value[channels:]
-
         def layer(x, c):
             part[x] = jnp.dot(w96[...], x9[t, x], preferred_element_type=F32)
             return c
@@ -195,7 +213,14 @@
     lax.fori_loop(0, slots, forward, 0)
 
     full_rows = rows_out * n_w
-    gain_wide = jnp.broadcast_to(gain[...], (rows_out, PLANE))
+    square = (rows_out, rows_out)
+    diagonal = lax.broadcasted_iota(jnp.int32, square, 0) == lax.broadcasted_iota(
+        jnp.int32, square, 1
+    )
+    column = jnp.sum(
+        jnp.where(diagonal, jnp.broadcast_to(gain[...], square), 0.0), axis=1, keepdims=True
+    )
+    gain_wide = jnp.broadcast_to(column, (rows_out, PLANE))
 
     def cell_terms(t, x):
         lanes = pl.ds(pl.multiple_of(x * PLANE, PLANE), PLANE)
@@ -203,7 +228,7 @@
         scaled = conv[t, x] * row
         normed = scaled * gain_wide
         s = jax.nn.sigmoid(normed)
-        grad = cot[t, :, lanes].astype(F32) * s * (1.0 + normed * (1.0 - s)) * act[t]
+        grad = cot[t, :, lanes].astype(F32) * s * (1.0 + normed * (1.0 - s)) * live(t)
         return lanes, row, scaled, normed, s, grad
 
     def middle(t, c):
@@ -216,7 +241,7 @@
 
         def cells(x, c):
             lanes, row, scaled, normed, s, grad = cell_terms(t, x)
-            out[t, :, lanes] = (normed * s * act[t]).astype(BF)
+            out[t, :, lanes] = (normed * s * live(t)).astype(BF)
             gacc[...] += grad * scaled
             grad_scaled = grad * gain_wide
             pf[pl.ds(x, 1)] = jnp.sum(grad_scaled * scaled, axis=0, keepdims=True)
@@ -323,21 +348,20 @@
     each(lambda d: gather(d, lax.rem(me_s + n_space - d, n_space)).wait_recv())
     each(lambda d: scatter(d).wait_send())
     each(lambda d: gather(d, me_s).wait_send())
-    red_out[...] = full[...]
+    for k in range(27):
+        dx, j = k // 9, k % 9
+        b, lane = j * channels // LANES, j * channels % LANES
+        top = b * rows + (2 - dx) * rows_out
+        weight_out[k] = full[top : top + rows_out, lane : lane + channels]
+    gain_out[...] = jnp.sum(
+        jnp.where(diagonal, full[at : at + rows_out, :rows_out], 0.0), axis=0, keepdims=True
+    )
 
 
 def shards(features, weights, gain, cotangent, counts, neighbors):
     slots, channels, cells = features.shape
     rows_out = weights.shape[1]
     n_space, n_w = lax.axis_size("space"), lax.axis_size("wshard")
-    slot_ids = jnp.arange(slots, dtype=jnp.int32)
-    active = slot_ids < counts[0]
-    local = jnp.where(neighbors >= 0, neighbors % slots, slots)
-    own = jnp.where(active, slot_ids, slots)[:, None]
-    idx = jnp.concatenate([local[:, :13], own, local[:, 13:]], axis=1).astype(jnp.int32)
-    w96 = weights.reshape(3, 9, rows_out, channels).transpose(0, 2, 1, 3).reshape(
-        3 * rows_out, 9 * channels
-    )
     perms, masks = shift_tables()
     rows = 3 * rows_out
     blocks = (9 * channels + LANES - 1) // LANES
@@ -346,15 +370,17 @@
     vmem = pl.BlockSpec(memory_space=pltpu.VMEM)
     smem = pl.BlockSpec(memory_space=pltpu.SMEM)
     dma = pltpu.SemaphoreType.DMA
-    out, red = pl.pallas_call(
+    out, weight_grad, gain_grad = pl.pallas_call(
         functools.partial(kernel, n_space, n_w),
         out_shape=(
             jax.ShapeDtypeStruct((slots, rows_out, cells), BF),
-            jax.ShapeDtypeStruct((red_rows, LANES), F32),
+            jax.ShapeDtypeStruct((27, rows_out, channels), F32),
+            jax.ShapeDtypeStruct((1, rows_out), F32),
         ),
         in_specs=[smem, smem, vmem, vmem, vmem, vmem, vmem, vmem],
-        out_specs=(vmem, vmem),
+        out_specs=(vmem, vmem, vmem),
         scratch_shapes=[
+            pltpu.VMEM((rows, 9 * channels), BF),
             pltpu.VMEM((slots + 1, TILE, channels, PLANE), BF),
             pltpu.VMEM((2, slots + 1, channels, PLANE), BF),
             pltpu.VMEM((2, slots, channels, PLANE), BF),
@@ -382,16 +408,10 @@
             collective_id=0, has_side_effects=True, vmem_limit_bytes=56 * 1024 * 1024
         ),
     )(
-        idx, active.astype(F32), features, w96, gain.reshape(rows_out, 1), cotangent,
+        neighbors, counts, features, weights, gain.reshape(1, rows_out), cotangent,
         jnp.asarray(perms, BF), jnp.asarray(masks, BF),
     )
-    taken = red[: blocks * rows].reshape(blocks, 3, rows_out, LANES)[:, ::-1]
-    taken = taken.transpose(1, 2, 0, 3).reshape(3, rows_out, blocks * LANES)[:, :, : 9 * channels]
-    weight_grad = taken.reshape(3, rows_out, 9, channels).transpose(0, 2, 1, 3).reshape(
-        27, rows_out, channels
-    )
-    gain_grad = red[blocks * rows : blocks * rows + rows_out, 0]
-    return (out, weight_grad, gain_grad)
+    return (out, weight_grad, gain_grad.reshape(rows_out))
 
 
 def solution(mesh):

time: 83.7 us -> 58 us (0.69)
  Pallas kernels: 72.3 us -> 52.9 us
  local copies, waits for them, and re-layouts: 7.9 us -> 3.62 us
  other arithmetic: 1.93 us -> 0 us
    pallas_call x1, Pallas kernels: 72.3 us -> 52.9 us  [shards(): pl.pallas_call(functools.partial(kernel, n_space, n_w), out_shape=(jax.Sh...]
    reshape x6 -> x0, local copies, waits for them, and re-layouts: 3.62 us -> none  [the longest x2 1.94 us: shards(): weights.reshape(3, 9, rows_out, channels).transpose(0, 2, 1, 3)]
    unnamed x3 -> x7, local copies, waits for them, and re-layouts: 0.97 us -> 3.62 us
    slice x3 -> x0, local copies, waits for them, and re-layouts: 2.38 us -> none  [the longest x1 1.34 us: shards(): gain_grad = red[blocks * rows:blocks * rows + rows_out, 0]]
    transpose x2 -> x0, local copies, waits for them, and re-layouts: 0.93 us -> none  [the longest x1 0.9 us: shards(): taken.reshape(3, rows_out, 9, channels).transpose(0, 2, 1, 3)]
where the time goes in v2:
time: 58 us; the launch traced here: 57.8 us
  Pallas kernels  52.9 us (91%)
  local copies, waits for them, and re-layouts  3.62 us (6%)
  between operations  1.3 us (2%)
    pallas_call x1, Pallas kernels, shards(): pl.pallas_call(functools.partial(kernel, n_space, n_w), out_shape=(jax.Sh...  52.9 us
    unnamed x7, local copies, waits for them, and re-layouts  3.62 us

profile of v2, /device:TPU:0, one launch (start us, length us, event | category | flops | bytes accessed | tf_op | source)
XLA Modules:
  0.0 57.8 jit_solution(13273625240675330345)
XLA Ops:
  1.3 52.9 %shard_map.103 = (bf16[4,32,4096]{2,1,0:T(8,128)(2,1)}, f32[27,32,64]{2,1,0:T(8,128)}, f32[1,32]{1,0:T(1,128)}) custom-call(s32[4,26]{1,0:T(4,128)} %neighbors.1, s32[1]{0:T(128)S(6)} %copy.14.counts, bf16[4,64,4096]{2,1,0:T(8,128)(2,1)} %feat.1, bf16[27,32,64]{2,1,0:T(8,128)(2,1)} %weights.1, f32[1,32]{1,0:T(1,128)} %bitcast.2, bf16[4,32,4096]{2,1,0:T(8,128)(2,1)} %cot.1, ...), custom_call_target="tpu_custom_call" | custom-call | tf_op jit(solution)/shard_map/pallas_call | solution.py:373
  54.2 0.0 copy-start
  54.2 0.0 copy-start.1
  54.2 2.3 %copy.15 = bf16[4,32,4096]{2,1,0:T(8,128)(2,1)} copy(bf16[4,32,4096]{2,1,0:T(8,128)(2,1)} %get-tuple-element.12) | data formatting | bytes 2097152
  56.5 0.0 copy-done
  56.6 0.8 %copy.16 = f32[27,32,64]{2,1,0:T(8,128)} copy(f32[27,32,64]{2,1,0:T(8,128)S(1)} %copy-done) | data formatting | bytes 442368
  57.3 0.0 copy-done.1
  57.3 0.5 copy.17
Async XLA Ops:
  54.2 2.4 %copy-start = (f32[27,32,64]{2,1,0:T(8,128)S(1)}, f32[27,32,64]{2,1,0:T(8,128)}, u32[]{:S(2)}) copy-start(f32[27,32,64]{2,1,0:T(8,128)} %get-tuple-element.13) | copy-start | bytes 663556
  54.2 3.1 %copy-start.1 = (f32[1,32]{1,0:T(1,128)S(1)}, f32[1,32]{1,0:T(1,128)}, u32[]{:S(2)}) copy-start(f32[1,32]{1,0:T(1,128)} %get-tuple-element.8) | copy-start | bytes 388

commit v3 on v2

--- a/solution.py
+++ b/solution.py
@@ -93,7 +93,6 @@
     for s in range(slots):
         sendp[0, s] = feat[s, :, (TILE - 1) * PLANE :]
         sendp[1, s] = feat[s, :, :PLANE]
-    pl.semaphore_wait(barrier, n_space - 1 + n_w - 1)
 
     def halo(side):
         step = 1 if side == 0 else n_space - 1
@@ -107,9 +106,6 @@
         )
 
     for side in range(2):
-        halo(side).start()
-
-    for side in range(2):
         edge[side, slots] = jnp.zeros((channels, PLANE), BF)
 
     def fill(x, c):
@@ -125,6 +121,11 @@
         w96[dx * rows_out : (dx + 1) * rows_out, j * channels : (j + 1) * channels] = weights[k]
     acc[...] = jnp.zeros_like(acc)
     gacc[...] = jnp.zeros_like(gacc)
+
+    pl.semaphore_wait(barrier, n_space - 1 + n_w - 1)
+
+    for side in range(2):
+        halo(side).start()
 
     GROUP = 16
 
@@ -193,7 +194,7 @@
             part[x] = jnp.dot(w96[...], x9[t, x], preferred_element_type=F32)
             return c
 
-        lax.fori_loop(0, TILE + 2, layer, 0, unroll=2)
+        lax.fori_loop(0, TILE + 2, layer, 0, unroll=6)
 
         def combine(x, c):
             value = (
@@ -205,7 +206,7 @@
             sq[0, t, pl.ds(x, 1)] = jnp.sum(value * value, axis=0, keepdims=True)
             return c
 
-        lax.fori_loop(0, TILE, combine, 0, unroll=2)
+        lax.fori_loop(0, TILE, combine, 0, unroll=4)
         for d in range(1, n_w):
             squares(t, d).start()
         return c
@@ -247,7 +248,7 @@
             pf[pl.ds(x, 1)] = jnp.sum(grad_scaled * scaled, axis=0, keepdims=True)
             return c
 
-        lax.fori_loop(0, TILE, cells, 0, unroll=2)
+        lax.fori_loop(0, TILE, cells, 0, unroll=4)
         pb[0, t] = pf[...].astype(BF)
         for d in range(1, n_w):
             sums(t, d).start()
@@ -272,16 +273,20 @@
             gz[x + 2] = value.astype(BF)
             return c
 
-        lax.fori_loop(0, TILE, cells, 0, unroll=2)
+        lax.fori_loop(0, TILE, cells, 0, unroll=4)
 
         def layer(x, c):
-            left = gz[pl.ds(x, 3)].reshape(3 * rows_out, PLANE)
-            acc[...] += lax.dot_general(
-                left, x9[t, x], (((1,), (1,)), ((), ())), preferred_element_type=F32
-            )
-            return c
-
-        lax.fori_loop(0, TILE + 2, layer, 0, unroll=2)
+            total = None
+            for step in range(6):
+                left = gz[pl.ds(6 * x + step, 3)].reshape(3 * rows_out, PLANE)
+                term = lax.dot_general(
+                    left, x9[t, 6 * x + step], (((1,), (1,)), ((), ())), preferred_element_type=F32
+                )
+                total = term if total is None else total + term
+            acc[...] += total
+            return c
+
+        lax.fori_loop(0, (TILE + 2) // 6, layer, 0)
         return c
 
     lax.fori_loop(0, slots, backward, 0)

time: 58 us -> 50.2 us (0.87)
  Pallas kernels: 52.9 us -> 45.1 us
    pallas_call x1, Pallas kernels: 52.9 us -> 45.1 us  [shards(): pl.pallas_call(functools.partial(kernel, n_space, n_w), out_shape=(jax.Sh...]
where the time goes in v3:
time: 50.2 us; the launch traced here: 50 us
  Pallas kernels  45.1 us (90%)
  local copies, waits for them, and re-layouts  3.62 us (7%)
  between operations  1.3 us (3%)
    pallas_call x1, Pallas kernels, shards(): pl.pallas_call(functools.partial(kernel, n_space, n_w), out_shape=(jax.Sh...  45.1 us
    unnamed x7, local copies, waits for them, and re-layouts  3.62 us

profile of v3, /device:TPU:0, one launch (start us, length us, event | category | flops | bytes accessed | tf_op | source)
XLA Modules:
  0.0 50.0 jit_solution(15130348994708497381)
XLA Ops:
  1.3 45.1 %shard_map.103 = (bf16[4,32,4096]{2,1,0:T(8,128)(2,1)}, f32[27,32,64]{2,1,0:T(8,128)}, f32[1,32]{1,0:T(1,128)}) custom-call(s32[4,26]{1,0:T(4,128)} %neighbors.1, s32[1]{0:T(128)S(6)} %copy.14.counts, bf16[4,64,4096]{2,1,0:T(8,128)(2,1)} %feat.1, bf16[27,32,64]{2,1,0:T(8,128)(2,1)} %weights.1, f32[1,32]{1,0:T(1,128)} %bitcast.2, bf16[4,32,4096]{2,1,0:T(8,128)(2,1)} %cot.1, ...), custom_call_target="tpu_custom_call" | custom-call | tf_op jit(solution)/shard_map/pallas_call | solution.py:378
  46.4 0.0 copy-start
  46.4 0.0 copy-start.1
  46.4 2.3 %copy.15 = bf16[4,32,4096]{2,1,0:T(8,128)(2,1)} copy(bf16[4,32,4096]{2,1,0:T(8,128)(2,1)} %get-tuple-element.12) | data formatting | bytes 2097152
  48.7 0.0 copy-done
  48.7 0.8 %copy.16 = f32[27,32,64]{2,1,0:T(8,128)} copy(f32[27,32,64]{2,1,0:T(8,128)S(1)} %copy-done) | data formatting | bytes 442368
  49.5 0.0 copy-done.1
  49.5 0.5 %copy.17 = f32[32]{0:T(128)} copy(f32[32]{0:T(128)S(1)} %bitcast.3) | data formatting | bytes 256
Async XLA Ops:
  46.4 2.4 %copy-start = (f32[27,32,64]{2,1,0:T(8,128)S(1)}, f32[27,32,64]{2,1,0:T(8,128)}, u32[]{:S(2)}) copy-start(f32[27,32,64]{2,1,0:T(8,128)} %get-tuple-element.13) | copy-start | bytes 663556
  46.4 3.1 %copy-start.1 = (f32[1,32]{1,0:T(1,128)S(1)}, f32[1,32]{1,0:T(1,128)}, u32[]{:S(2)}) copy-start(f32[1,32]{1,0:T(1,128)} %get-tuple-element.8) | copy-start | bytes 388
